TPU v7x, 32 devices: a whole 2x2x4 slice. The times are simulated.
32 devices in a mesh: dp: 8 (over z, core), cp: 4 (over y, x).
Axes of the slice: x: 2, y: 2, z: 4, core: 2. Of those that a mesh axis runs over, the one named last changes fastest.
Arguments:
- queries: bfloat16 [4096, 3072], P(('dp', 'cp')), may hold values from -48 to 48
- key_heads: bfloat16 [4096, 512], P(('dp', 'cp')), may hold values from -6 to 6
- value_heads: bfloat16 [4096, 512], P(('dp', 'cp')), may hold values from -6 to 6
- segment_ids: int32 [8, 512], P('dp', 'cp'), may hold values from 0 to 1, never falling along the last dimension, each value on 1 to 384 neighbouring positions
- out_weight: bfloat16 [3072, 3072], P('dp', 'cp'), may hold values from -0.109375 to 0.109375
- grad_out: bfloat16 [4096, 3072], P('dp', 'cp'), may hold values from -6 to 6
Outputs:
- output: bfloat16 [4096, 3072], P('dp', 'cp')
- grad_queries: bfloat16 [4096, 3072], P(('dp', 'cp'))
- grad_keys: bfloat16 [4096, 512], P(('dp', 'cp'))
- grad_values: bfloat16 [4096, 512], P(('dp', 'cp'))
- grad_weight: float32 [3072, 3072], P('dp', 'cp')
Inputs may be any that keep to these rules, and one draw needn't show every extreme that they name: `segment_ids`: document numbers of a group never fall; a document holds at most 384 positions.
All inputs are finite; a program needn't handle non-finite values.
Results may differ from a plain program's by a relative error of at most 0.023.
Values may be sent and summed in bfloat16 or wider, within the bound.
A program may use at most 128 MiB of HBM per device.

v0:
```python
import math

import jax
import jax.numpy as jnp
from jax import lax
from jax.sharding import PartitionSpec as P

HQ = 24
HK = 4
HD = 128


def masked_logits(query_tiles, query_pos, own_segment, key_block, segment_block):
    count_rows = key_block.shape[0]
    key_tiles = key_block.reshape(count_rows, HK, HD)
    logits = jnp.einsum(
        "qhrd,khd->hrqk", query_tiles, key_tiles, preferred_element_type=jnp.float32
    ) * (1.0 / math.sqrt(HD))
    key_pos = jnp.arange(count_rows, dtype=jnp.int32)
    allowed = (own_segment[:, None] == segment_block[None, :]) & (
        key_pos[None, :] <= query_pos[:, None]
    )
    return (jnp.where(allowed, logits, -1e30), allowed)


def per_device(queries, key_heads, value_heads, segment_ids, out_weight, grad_out):
    rows_own = queries.shape[0]
    head_share = HQ // HK
    kv_width = key_heads.shape[1]
    score_scale = 1.0 / math.sqrt(HD)
    weight_cols = lax.all_gather(out_weight, "dp", axis=0, tiled=True)
    grad_rows = grad_out
    grad_attended = lax.psum_scatter(
        lax.dot_general(
            grad_rows, weight_cols, (((1,), (1,)), ((), ())), preferred_element_type=jnp.float32
        ),
        "cp",
        scatter_dimension=0,
        tiled=True,
    ).astype(jnp.bfloat16)
    query_tiles = queries.reshape(rows_own, HK, head_share, HD)
    grad_tiles = grad_attended.reshape(rows_own, HK, head_share, HD)
    query_pos = lax.axis_index("cp") * rows_own + jnp.arange(rows_own, dtype=jnp.int32)
    own_segment = segment_ids[0].astype(jnp.bfloat16)

    def logits_of(blocks):
        return masked_logits(query_tiles, query_pos, own_segment, blocks[0], blocks[-1])

    def probability_of(softmax_stats, blocks):
        logits, allowed = logits_of(blocks)
        weights = jnp.where(allowed, jnp.exp(logits - softmax_stats[0][..., None]), 0.0)
        return weights / softmax_stats[1][..., None]

    row_peak = jnp.full((HK, head_share, rows_own), -1e30, jnp.float32)
    logits, allowed = logits_of(
        (
            lax.all_gather(key_heads, "cp", axis=0, tiled=True),
            lax.all_gather(own_segment, "cp", axis=0, tiled=True),
        )
    )
    new_peak = jnp.maximum(row_peak, jnp.max(logits, axis=-1))
    kept_terms = jnp.where(allowed, jnp.exp(logits - new_peak[..., None]), 0.0)
    softmax_stats = (new_peak, jnp.sum(kept_terms, axis=-1))
    blocks = (
        lax.all_gather(key_heads, "cp", axis=0, tiled=True),
        lax.all_gather(value_heads, "cp", axis=0, tiled=True),
        lax.all_gather(own_segment, "cp", axis=0, tiled=True),
    )
    count_rows = blocks[1].shape[0]
    value_tiles = blocks[1].reshape(count_rows, HK, HD)
    probability = probability_of(softmax_stats, blocks)
    rounded_prob = probability.astype(jnp.bfloat16)
    value_acc = jnp.einsum(
        "hrqk,khd->qhrd", rounded_prob, value_tiles, preferred_element_type=jnp.float32
    )
    grad_prob = jnp.einsum(
        "qhrd,khd->hrqk", grad_tiles, value_tiles, preferred_element_type=jnp.float32
    )
    value_acc, delta_sum = (value_acc, jnp.sum(probability * grad_prob, axis=-1))
    blocks = (
        lax.all_gather(key_heads, "cp", axis=0, tiled=True),
        lax.all_gather(value_heads, "cp", axis=0, tiled=True),
        lax.all_gather(own_segment, "cp", axis=0, tiled=True),
    )
    count_rows = blocks[0].shape[0]
    key_tiles = blocks[0].reshape(count_rows, HK, HD)
    value_tiles = blocks[1].reshape(count_rows, HK, HD)
    probability = probability_of(softmax_stats, blocks)
    rounded_prob = probability.astype(jnp.bfloat16)
    grad_prob = jnp.einsum(
        "qhrd,khd->hrqk", grad_tiles, value_tiles, preferred_element_type=jnp.float32
    )
    grad_logit = (probability * (grad_prob - delta_sum[..., None])).astype(jnp.bfloat16)
    grad_query_acc = jnp.einsum(
        "hrqk,khd->qhrd", grad_logit, key_tiles, preferred_element_type=jnp.float32
    )
    key_part = (
        jnp.einsum("hrqk,qhrd->khd", grad_logit, query_tiles, preferred_element_type=jnp.float32)
        * score_scale
    ).reshape(count_rows, kv_width)
    value_part = jnp.einsum(
        "hrqk,qhrd->khd", rounded_prob, grad_tiles, preferred_element_type=jnp.float32
    ).reshape(count_rows, kv_width)
    key_grad_all = key_part
    value_grad_all = value_part
    grad_query_acc, key_grad_all, value_grad_all = (grad_query_acc, key_grad_all, value_grad_all)
    attended = value_acc.astype(jnp.bfloat16).reshape(rows_own, -1)
    attended_block = lax.all_gather(attended, "cp", axis=0, tiled=True)
    out_all = jnp.dot(attended_block, weight_cols, preferred_element_type=jnp.float32)
    grad_rows = grad_out
    weight_partial = lax.dot_general(
        attended_block, grad_rows, (((0,), (0,)), ((), ())), preferred_element_type=jnp.float32
    )
    out_all, weight_partial = (out_all, weight_partial)
    grad_weight = lax.psum_scatter(
        weight_partial.astype(jnp.bfloat16), "dp", scatter_dimension=0, tiled=True
    ).astype(jnp.float32)
    key_sums, value_sums = (
        lax.psum_scatter(key_grad_all, "cp", scatter_dimension=0, tiled=True),
        lax.psum_scatter(value_grad_all, "cp", scatter_dimension=0, tiled=True),
    )
    grad_queries = (grad_query_acc * score_scale).astype(jnp.bfloat16).reshape(rows_own, -1)
    return (
        out_all.astype(jnp.bfloat16),
        grad_queries,
        key_sums.astype(jnp.bfloat16),
        value_sums.astype(jnp.bfloat16),
        grad_weight,
    )


def solution(mesh):
    in_specs = (
        P(("dp", "cp"), None),
        P(("dp", "cp"), None),
        P(("dp", "cp"), None),
        P("dp", "cp"),
        P("dp", "cp"),
        P("dp", "cp"),
    )
    out_specs = (
        P("dp", "cp"),
        P(("dp", "cp"), None),
        P(("dp", "cp"), None),
        P(("dp", "cp"), None),
        P("dp", "cp"),
    )
    return jax.shard_map(
        per_device, mesh=mesh, in_specs=in_specs, out_specs=out_specs, check_vma=False
    )
```

profile of v0, /device:TPU:0, one launch (start us, length us, event | category | flops | bytes accessed | tf_op | source)
XLA Modules:
  0.0 307.7 jit_solution(13074188611589706599)
XLA Ops:
  7.2 0.7 all-gather.6.cloned.1.call-update
  8.0 1.0 copy.26
  9.0 11.8 %all_gather.22 = bf16[512,512]{1,0:T(8,128)(2,1)S(1)} all-gather(bf16[128,512]{1,0:T(8,128)(2,1)} %param.8), channel_id=1, replica_groups=mesh['dp'=8,'cp'=4] {'cp'}, dimensions={0}, use_global_device_ids=true | all-gather | bytes 655360 | tf_op jit(solution)/shard_map/all_gather | solution.py:66
  21.1 1.7 copy.27
  23.4 7.7 %all-gather = bf16[1,512]{1,0:T(2,128)(2,1)S(1)} all-gather(bf16[1,128]{1,0:T(2,128)(2,1)S(1)} %get-tuple-element.15), channel_id=2, replica_groups=mesh['dp'=8,'cp'=4] {'cp'}, dimensions={1}, use_global_device_ids=true | all-gather | bytes 1280 | tf_op jit(solution)/shard_map/all_gather | solution.py:67
  31.2 9.3 %all_gather.21 = bf16[512,512]{0,1:T(8,128)(2,1)S(1)} all-gather(bf16[128,512]{0,1:T(8,128)(2,1)S(1)} %copy.26), channel_id=1, replica_groups=mesh['dp'=8,'cp'=4] {'cp'}, dimensions={0}, use_global_device_ids=true | all-gather | bytes 655360 | tf_op jit(solution)/shard_map/all_gather | solution.py:65
  40.6 1.1 fusion.3
  41.7 1.5 fusion.5
  43.3 2.9 fusion.10
  46.3 17.8 %all-gather.6.cloned.1.call-done = bf16[3072,768]{1,0:T(8,128)(2,1)} async-done(((bf16[384,768]{1,0:T(8,128)(2,1)}), bf16[3072,768]{1,0:T(8,128)(2,1)}) %all-gather.6.cloned.1.call-update) | async-done | bytes 4718608 | tf_op jit(solution)/shard_map/all_gather | solution.py:31
  64.1 6.8 %fusion.18 = f32[512,3072]{1,0:T(8,128)} fusion(bf16[512,768]{1,0:T(8,128)(2,1)S(1)} %copy-done, bf16[3072,768]{1,0:T(8,128)(2,1)} %all-gather.6.cloned.1.call-done), kind=kOutput, calls=%fused_computation.26 | convolution fusion | flops 2415919104 | bytes 11796480 | tf_op jit(solution)/shard_map/dot_general | solution.py:34
  71.0 38.2 %all-gather.4.cloned.1.call-done = bf16[512,3072]{0,1:T(8,128)(2,1)} async-done(((bf16[128,3072]{0,1:T(8,128)(2,1)}), bf16[512,3072]{0,1:T(8,128)(2,1)}) %all-gather.4.cloned.1.call-update) | async-done | bytes 3145744 | tf_op jit(solution)/shard_map/all_gather | solution.py:108
  109.2 6.7 %convolution_convert_fusion = bf16[3072,768]{1,0:T(8,128)(2,1)} fusion(bf16[512,3072]{0,1:T(8,128)(2,1)} %all-gather.4.cloned.1.call-done, bf16[512,768]{1,0:T(8,128)(2,1)S(1)} %copy-done), kind=kOutput, calls=%fused_computation.8 | convolution fusion | flops 2418278400 | bytes 8650752 | tf_op jit(solution)/shard_map/dot_general | solution.py:111
  116.1 66.3 %reduce-scatter.5.cloned.1.call-done = f32[128,3072]{1,0:T(8,128)} async-done(((f32[512,3072]{1,0:T(8,128)}), f32[128,3072]{1,0:T(8,128)}) %reduce-scatter.5.cloned.1.call-update) | async-done | bytes 1572880 | tf_op jit(solution)/shard_map/reduce_scatter | solution.py:33
  182.4 1.5 convert_element_type.53
  183.9 1.2 copy.32
  185.1 5.0 %fusion.6 = f32[4,128,512,1]{2,1,3,0:T(8,128)S(1)} fusion(bf16[128,4,6,128]{0,3,2,1:T(8,128)(2,1)} %bitcast.93, f32[4,512,128,6]{2,1,3,0:T(8,128)} %copy-done.1, f32[4,6,128]{2,1,0:T(8,128)S(1)} %fusion.5, f32[4,6,128]{2,1,0:T(8,128)S(1)} %broadcast_maximum_fusion, pred[128,512]{0,1:T(8,128)(4,1)S(1)} %fusion.14), kind=kOutput, calls=%fused_computation.12 | convolution fusion | flops 412090368 | bytes 8216576 | tf_op jit(solution)/shard_map/hrqk,qhrd->khd/dot_general | solution.py:101
  190.1 1.3 copy.40
  191.5 5.6 %fusion = (f32[4,6,128]{2,1,0:T(8,128)S(1)}, f32[4,128,6,512]{1,3,2,0:T(8,128)S(1)}) fusion(f32[4,6,128]{2,1,0:T(8,128)S(1)} %fusion.5, f32[4,6,128]{2,1,0:T(8,128)S(1)} %broadcast_maximum_fusion, f32[4,512,128,6]{2,1,3,0:T(8,128)} %copy-done.1, pred[128,512]{0,1:T(8,128)(4,1)S(1)} %fusion.14, bf16[128,4,6,128]{0,3,2,1:T(8,128)(2,1)} %bitcast.94, ...), kind=kOutput, calls=%fused_computation.2 | convolution fusion | flops 413660160 | bytes 13996032 | tf_op jit(solution)/shard_map/qhrd,khd->hrqk/dot_general | solution.py:90
  197.1 4.1 %fusion.2 = bf16[4,6,128,512]{2,3,1,0:T(8,128)(2,1)S(1)} fusion(f32[4,128,6,512]{1,3,2,0:T(8,128)S(1)} %get-tuple-element.20, f32[4,6,128]{2,1,0:T(8,128)S(1)} %get-tuple-element.19, f32[4,6,128]{2,1,0:T(8,128)S(1)} %fusion.5, f32[4,6,128]{2,1,0:T(8,128)S(1)} %broadcast_maximum_fusion, f32[4,512,128,6]{2,1,3,0:T(8,128)} %copy-done.1, ...), kind=kLoop, calls=%fused_computation.4 | loop fusion | flops 12582912 | bytes 15831040 | tf_op jit(solution)/shard_map/convert_element_type | solution.py:93
  201.2 1.6 copy-done.2
  202.9 1.1 fusion.13
  204.0 1.3 copy.38
  205.3 6.9 %convolution_convert_fusion.1 = bf16[512,768]{1,0:T(8,128)(2,1)} fusion(bf16[512,3072]{0,1:T(8,128)(2,1)} %all-gather.4.cloned.1.call-done, bf16[3072,768]{1,0:T(8,128)(2,1)} %all-gather.6.cloned.1.call-done), kind=kOutput, calls=%fused_computation.17 | convolution fusion | flops 2416312320 | bytes 8650752 | tf_op jit(solution)/shard_map/dot_general | solution.py:109
  212.3 27.3 %reduce-scatter.11.cloned.1.call-done = bf16[384,768]{1,0:T(8,128)(2,1)} async-done(((bf16[3072,768]{1,0:T(8,128)(2,1)}), bf16[384,768]{1,0:T(8,128)(2,1)}) %reduce-scatter.11.cloned.1.call-update) | async-done | bytes 589840 | tf_op jit(solution)/shard_map/reduce_scatter | solution.py:115
  239.6 2.2 convert_element_type.60
  241.7 2.5 multiply_convert_fusion
  244.3 1.2 copy.41
  245.4 23.0 %reduce-scatter.9.cloned.1.call-done = f32[128,512]{1,0:T(8,128)} async-done(((f32[512,512]{1,0:T(8,128)}), f32[128,512]{1,0:T(8,128)}) %reduce-scatter.9.cloned.1.call-update) | async-done | bytes 262160 | tf_op jit(solution)/shard_map/reduce_scatter | solution.py:120
  268.4 1.6 convert_element_type.58
  270.1 29.1 %reduce-scatter.7.cloned.1.call-done = f32[128,512]{1,0:T(8,128)} async-done(((f32[512,512]{1,0:T(8,128)}), f32[128,512]{1,0:T(8,128)}) %reduce-scatter.7.cloned.1.call-update) | async-done | bytes 262160 | tf_op jit(solution)/shard_map/reduce_scatter | solution.py:119
  299.2 1.6 convert_element_type.57
  (24 shorter events, 1.6 us)
Async XLA Ops:
  7.2 56.9 %copy-start = (bf16[512,768]{1,0:T(8,128)(2,1)S(1)}, bf16[512,768]{1,0:T(8,128)(2,1)}, u32[]{:S(2)}) copy-start(bf16[512,768]{1,0:T(8,128)(2,1)} %param.11) | copy-start | bytes 2359300
  7.2 56.9 %all-gather.6.cloned.1.call-start = ((), (), s32[]{:S(2)}) async-start(), calls=%async_computation.5 | async-start | bytes 5308416 | tf_op jit(solution)/shard_map/all_gather | solution.py:31
  7.9 101.3 %all-gather.4.cloned.1.call-start = ((), (), s32[]{:S(2)}) async-start(), calls=%async_computation.4 | async-start | bytes 3932160 | tf_op jit(solution)/shard_map/all_gather | solution.py:108
  21.1 22.2 %copy-start.3 = (bf16[512,512]{0,1:T(8,128)(2,1)}, bf16[512,512]{0,1:T(8,128)(2,1)S(1)}, u32[]{:S(2)}) copy-start(bf16[512,512]{0,1:T(8,128)(2,1)S(1)} %copy.30) | copy-start | bytes 1572868
  41.7 4.5 %copy-start.1 = (f32[4,512,128,6]{2,1,3,0:T(8,128)}, f32[4,512,128,6]{2,1,3,0:T(8,128)S(1)}, u32[]{:S(2)}) copy-start(f32[4,512,128,6]{2,1,3,0:T(8,128)S(1)} %get-tuple-element.18) | copy-start | bytes 18874372
  46.2 136.2 %reduce-scatter.5.cloned.1.call-start = ((), (), s32[]{:S(2)}) async-start(), calls=%async_computation.6 | async-start | bytes 7864320 | tf_op jit(solution)/shard_map/reduce_scatter | solution.py:33
  70.9 168.6 %reduce-scatter.11.cloned.1.call-start = ((), (), s32[]{:S(2)}) async-start(), calls=%async_computation.9 | async-start | bytes 5308416 | tf_op jit(solution)/shard_map/reduce_scatter | solution.py:115
  115.9 152.6 %reduce-scatter.9.cloned.1.call-start = ((), (), s32[]{:S(2)}) async-start(), calls=%async_computation.8 | async-start | bytes 1310720 | tf_op jit(solution)/shard_map/reduce_scatter | solution.py:120
  191.5 107.7 %reduce-scatter.7.cloned.1.call-start = ((), (), s32[]{:S(2)}) async-start(), calls=%async_computation.7 | async-start | bytes 1310720 | tf_op jit(solution)/shard_map/reduce_scatter | solution.py:119
  201.2 1.7 copy-start.2
Sparse Core Ops, SparseCore 0:
  9.7 54.3 all-gather.5
  66.5 42.6 all-gather.3
  112.2 70.2 reduce-scatter.4
  184.6 54.9 reduce-scatter.10
  242.3 26.0 reduce-scatter.8
  271.4 27.7 reduce-scatter.6
where the time goes:
time: 308 us
  waiting for transfers between devices  203 us (66%)
  matrix products  38.6 us (13%)
  blocking collectives  28.8 us (9%)
  between operations  14.3 us (5%)
  other arithmetic  13.4 us (4%)
  local copies, waits for them, and re-layouts  9.56 us (3%)
    reduce_scatter x1, waiting for transfers between devices, per_device(): lax.psum_scatter(lax.dot_general(grad_rows, weight_cols, (((1,), (1,)), (...  66.3 us
    all_gather x1, waiting for transfers between devices, per_device(): attended_block = lax.all_gather(attended, 'cp', axis=0, tiled=True)  38.2 us
    reduce_scatter x1, waiting for transfers between devices, per_device(): lax.psum_scatter(key_grad_all, 'cp', scatter_dimension=0, tiled=True)  29.1 us
    reduce_scatter x1, waiting for transfers between devices, per_device(): lax.psum_scatter(weight_partial.astype(jnp.bfloat16), 'dp', scatter_dimen...  27.3 us
    reduce_scatter x1, waiting for transfers between devices, per_device(): lax.psum_scatter(value_grad_all, 'cp', scatter_dimension=0, tiled=True)  23 us
    all_gather x1, waiting for transfers between devices, per_device(): weight_cols = lax.all_gather(out_weight, 'dp', axis=0, tiled=True)  17.8 us
    all_gather x1, blocking collectives, per_device(): lax.all_gather(value_heads, 'cp', axis=0, tiled=True)  11.8 us
    all_gather x1, blocking collectives, per_device(): lax.all_gather(key_heads, 'cp', axis=0, tiled=True)  9.26 us
  transfers between devices with their start and end apart: 6, of which 6 were waited for; matrix products, arithmetic and copies ran while one was open for 19% of the time, Pallas kernels for 0%

commit v1 on v0

v1 whole, which is shorter than its diff:
```python
import math

import jax
import jax.numpy as jnp
from jax import lax
from jax.sharding import PartitionSpec as P

HQ = 24
HK = 4
HD = 128


def per_device(queries, key_heads, value_heads, segment_ids, out_weight, grad_out):
    rows = queries.shape[0]
    n_cp = lax.axis_size("cp")
    group = rows * n_cp
    share = HQ // n_cp
    copies = n_cp // HK
    width = share * HD
    scale = 1.0 / math.sqrt(HD)
    f32 = jnp.float32
    bf16 = jnp.bfloat16
    weight_cols = lax.all_gather(out_weight, "dp", axis=0, tiled=True)
    packed = jnp.concatenate(
        [
            queries.reshape(rows, n_cp, width),
            jnp.repeat(key_heads.reshape(rows, HK, HD), copies, axis=1),
            jnp.repeat(value_heads.reshape(rows, HK, HD), copies, axis=1),
            jnp.broadcast_to(segment_ids[0].astype(bf16)[:, None, None], (rows, n_cp, HD)),
        ],
        axis=2,
    ).transpose(1, 0, 2)
    packed = lax.all_to_all(packed, "cp", 0, 0, tiled=True).reshape(group, -1)
    q = packed[:, :width].reshape(group, share, HD)
    k = packed[:, width : width + HD]
    v = packed[:, width + HD : width + 2 * HD]
    seg = packed[:, width + 2 * HD]
    pos = jnp.arange(group, dtype=jnp.int32)
    allowed = (seg[:, None] == seg[None, :]) & (pos[None, :] <= pos[:, None])
    logits = jnp.einsum("qrd,kd->rqk", q, k, preferred_element_type=f32) * scale
    logits = jnp.where(allowed, logits, -1e30)
    weights = jnp.exp(logits - jnp.max(logits, axis=-1, keepdims=True))
    weights = jnp.where(allowed, weights, 0.0)
    prob = weights / jnp.sum(weights, axis=-1, keepdims=True)
    rounded = prob.astype(bf16)
    attended = jnp.einsum("rqk,kd->qrd", rounded, v, preferred_element_type=f32)
    attended = attended.astype(bf16).reshape(group, width)
    attended_all = lax.all_gather(attended, "cp", axis=1, tiled=True)
    weight_partial = lax.dot_general(
        attended_all, grad_out, (((0,), (0,)), ((), ())), preferred_element_type=f32
    ).astype(bf16)
    grad_weight = lax.psum_scatter(weight_partial, "dp", scatter_dimension=0, tiled=True)
    part = lax.dot_general(
        grad_out, weight_cols, (((1,), (1,)), ((), ())), preferred_element_type=f32
    ).astype(bf16)
    ga = lax.psum_scatter(part, "cp", scatter_dimension=1, tiled=True)
    ga = ga.reshape(group, share, HD)
    grad_prob = jnp.einsum("qrd,kd->rqk", ga, v, preferred_element_type=f32)
    delta = jnp.sum(prob * grad_prob, axis=-1, keepdims=True)
    ds = (prob * (grad_prob - delta)).astype(bf16)
    dq = (jnp.einsum("rqk,kd->qrd", ds, k, preferred_element_type=f32) * scale).astype(bf16)
    dk = (jnp.einsum("rqk,qrd->kd", ds, q, preferred_element_type=f32) * scale).astype(bf16)
    dv = jnp.einsum("rqk,qrd->kd", rounded, ga, preferred_element_type=f32).astype(bf16)
    back = jnp.concatenate([dq.reshape(group, width), dk, dv], axis=1)
    back = lax.all_to_all(back.reshape(n_cp, rows, -1), "cp", 0, 0, tiled=True)
    back = back.transpose(1, 0, 2)
    summed = back[:, :, width:].reshape(rows, HK, copies, 2 * HD)
    summed = jnp.sum(summed.astype(f32), axis=2).astype(bf16)
    out = jnp.dot(attended_all, weight_cols, preferred_element_type=f32).astype(bf16)
    return (
        out,
        back[:, :, :width].reshape(rows, -1),
        summed[:, :, :HD].reshape(rows, -1),
        summed[:, :, HD:].reshape(rows, -1),
        grad_weight.astype(f32),
    )


def solution(mesh):
    rows = P(("dp", "cp"), None)
    grid = P("dp", "cp")
    return jax.shard_map(
        per_device,
        mesh=mesh,
        in_specs=(rows, rows, rows, grid, grid, grid),
        out_specs=(grid, rows, rows, rows, grid),
        check_vma=False,
    )
```

time: 308 us -> 225 us (0.73)
  waiting for transfers between devices: 203 us -> 128 us
  blocking collectives: 28.8 us -> 20.5 us
  other arithmetic: 13.4 us -> 5.95 us
  matrix products: 38.6 us -> 42.9 us
  starting transfers between devices: 0.42 us -> 3.86 us
    reduce_scatter x4 -> x2, waiting for transfers between devices: 146 us -> 66.7 us  [the longest x1 40.3 us: per_device(): ga = lax.psum_scatter(part, 'cp', scatter_dimension=1, tiled=True)]
    all_gather x3 -> x0, blocking collectives: 28.8 us -> none  [the longest x1 11.8 us: per_device(): lax.all_gather(value_heads, 'cp', axis=0, tiled=True)]
    all_to_all x0 -> x1, blocking collectives: none -> 20.5 us  [per_device(): packed = lax.all_to_all(packed, 'cp', 0, 0, tiled=True).reshape(group, -1)]
    convert_element_type x6 -> x3, other arithmetic: 11.7 us -> 4.58 us  [the longest x1 2.15 us: per_device(): grad_weight.astype(f32)]
    sub x0 -> x1, matrix products: none -> 5.43 us  [per_device(): weights = jnp.exp(logits - jnp.max(logits, axis=-1, keepdims=True))]
    all_gather x1, waiting for transfers between devices: 17.8 us -> 22 us  [per_device(): weight_cols = lax.all_gather(out_weight, 'dp', axis=0, tiled=True)]
    all_to_all x0 -> x1, starting transfers between devices: none -> 3.52 us  [per_device(): back = lax.all_to_all(back.reshape(n_cp, rows, -1), 'cp', 0, 0, tiled=True)]
    dot_general x9 -> x8, matrix products: 38.6 us -> 37.4 us  [the longest x1 6.9 us: per_device(): jnp.dot(attended_all, weight_cols, preferred_element_type=f32).astype(bf16)]
  transfers between devices with their start and end apart: 6 -> 5, of which waited for: 6 -> 4; matrix products, arithmetic and copies ran while one was open for 19% -> 24% of each run, Pallas kernels for 0% -> 0%
where the time goes in v1:
time: 225 us
  waiting for transfers between devices  128 us (57%)
  matrix products  42.9 us (19%)
  blocking collectives  20.5 us (9%)
  between operations  14 us (6%)
  local copies, waits for them, and re-layouts  9.72 us (4%)
  other arithmetic  5.95 us (3%)
  starting transfers between devices  3.86 us (2%)
    reduce_scatter x1, waiting for transfers between devices, per_device(): ga = lax.psum_scatter(part, 'cp', scatter_dimension=1, tiled=True)  40.3 us
    all_gather x1, waiting for transfers between devices, per_device(): attended_all = lax.all_gather(attended, 'cp', axis=1, tiled=True)  38.7 us
    reduce_scatter x1, waiting for transfers between devices, per_device(): lax.psum_scatter(weight_partial, 'dp', scatter_dimension=0, tiled=True)  26.4 us
    all_gather x1, waiting for transfers between devices, per_device(): weight_cols = lax.all_gather(out_weight, 'dp', axis=0, tiled=True)  22 us
    all_to_all x1, blocking collectives, per_device(): packed = lax.all_to_all(packed, 'cp', 0, 0, tiled=True).reshape(group, -1)  20.5 us
    dot_general x1, matrix products, per_device(): jnp.dot(attended_all, weight_cols, preferred_element_type=f32).astype(bf16)  6.9 us
    dot_general x1, matrix products, per_device(): lax.dot_general(attended_all, grad_out, (((0,), (0,)), ((), ())), preferr...  6.71 us
    dot_general x1, matrix products, per_device(): lax.dot_general(grad_out, weight_cols, (((1,), (1,)), ((), ())), preferre...  6.32 us
  transfers between devices with their start and end apart: 5, of which 4 were waited for; matrix products, arithmetic and copies ran while one was open for 24% of the time, Pallas kernels for 0%

profile of v1, /device:TPU:0, one launch (start us, length us, event | category | flops | bytes accessed | tf_op | source)
XLA Modules:
  0.0 224.9 jit_solution(4785272398331840322)
XLA Ops:
  7.2 0.7 all-gather.5.cloned.1.call-update
  8.0 1.2 copy.78
  9.2 0.7 convert_bitcast_fusion
  9.8 1.0 copy_bitcast_fusion.1
  11.0 20.5 %all_to_all.10 = bf16[4,128,1152]{2,1,0:T(8,128)(2,1)S(1)} all-to-all(bf16[4,128,1152]{2,1,0:T(8,128)(2,1)S(1)} %maximum_bitcast_fusion), channel_id=1, replica_groups=mesh['dp'=8,'cp'=4] {'cp'}, dimensions={0} | all-to-all | bytes 2359296 | tf_op jit(solution)/shard_map/all_to_all | solution.py:33
  31.6 0.3 copy.46
  32.0 0.2 fusion.24
  32.2 5.4 %fusion.32 = (f32[6,512]{1,0:T(8,128)S(1)}, f32[6,512,512]{1,2,0:T(8,128)}) fusion(pred[512,512]{0,1:T(8,128)(4,1)S(1)} %fusion.24, bf16[512,6,128]{0,2,1:T(8,128)(2,1)S(1)} %bitcast.111, bf16[512,1152]{1,0:T(8,128)(2,1)S(1)} %bitcast.102), kind=kOutput, calls=%fused_computation.45 | convolution fusion | flops 410518016 | bytes 7745536 | tf_op jit(solution)/shard_map/sub | solution.py:42
  37.7 4.4 %fusion.12 = bf16[128,6,512]{2,0,1:T(8,128)(2,1)} fusion(bf16[512,1152]{1,0:T(8,128)(2,1)S(1)} %bitcast.103, f32[6,512,512]{1,2,0:T(8,128)} %get-tuple-element.13, f32[6,512]{1,0:T(8,128)S(1)} %get-tuple-element.12), kind=kOutput, calls=%fused_computation.20 | convolution fusion | flops 406192128 | bytes 7225344 | tf_op jit(solution)/shard_map/rqk,kd->qrd/dot_general | solution.py:46
  42.1 22.0 %all-gather.5.cloned.1.call-done = bf16[3072,768]{1,0:T(8,128)(2,1)} async-done(((bf16[384,768]{1,0:T(8,128)(2,1)}), bf16[3072,768]{1,0:T(8,128)(2,1)}) %all-gather.5.cloned.1.call-update) | async-done | bytes 4718608 | tf_op jit(solution)/shard_map/all_gather | solution.py:23
  64.1 6.3 %convolution_convert_fusion.1 = bf16[512,3072]{1,0:T(8,128)(2,1)} fusion(bf16[512,768]{1,0:T(8,128)(2,1)S(1)} %copy-done, bf16[3072,768]{1,0:T(8,128)(2,1)} %all-gather.5.cloned.1.call-done), kind=kOutput, calls=%fused_computation.10 | convolution fusion | flops 2417491968 | bytes 8650752 | tf_op jit(solution)/shard_map/dot_general | solution.py:53
  70.4 0.2 reduce-scatter.5.cloned.1.call-start
  70.7 38.7 %all-gather.3.cloned.1.call-done = bf16[512,3072]{0,1:T(8,128)(2,1)} async-done(((bf16[512,768]{0,1:T(8,128)(2,1)}), bf16[512,3072]{0,1:T(8,128)(2,1)}) %all-gather.3.cloned.1.call-update) | async-done | bytes 3145744 | tf_op jit(solution)/shard_map/all_gather | solution.py:48
  109.3 6.7 %convolution_convert_fusion = bf16[3072,768]{1,0:T(8,128)(2,1)} fusion(bf16[512,3072]{0,1:T(8,128)(2,1)} %all-gather.3.cloned.1.call-done, bf16[512,768]{1,0:T(8,128)(2,1)S(1)} %copy-done), kind=kOutput, calls=%fused_computation.8 | convolution fusion | flops 2418278400 | bytes 8650752 | tf_op jit(solution)/shard_map/dot_general | solution.py:49
  116.1 40.3 %reduce-scatter.3.cloned.1.call-done = bf16[512,768]{1,0:T(8,128)(2,1)} async-done(((bf16[512,3072]{1,0:T(8,128)(2,1)}), bf16[512,768]{1,0:T(8,128)(2,1)}) %reduce-scatter.3.cloned.1.call-update) | async-done | bytes 786448 | tf_op jit(solution)/shard_map/reduce_scatter | solution.py:56
  156.3 1.4 copy.50
  157.7 4.0 %fusion.20 = bf16[512,128]{1,0:T(8,128)(2,1)S(1)} fusion(bf16[512,6,128]{0,2,1:T(8,128)(2,1)S(1)} %bitcast.114, f32[6,512,512]{1,2,0:T(8,128)} %get-tuple-element.13, f32[6,512]{1,0:T(8,128)S(1)} %get-tuple-element.12), kind=kOutput, calls=%fused_computation.27 | convolution fusion | flops 405864448 | bytes 7221248 | tf_op jit(solution)/shard_map/rqk,qrd->kd/dot_general | solution.py:63
  162.0 4.6 %fusion.1 = (f32[6,512]{1,0:T(8,128)S(1)}, f32[512,512,6]{1,0,2:T(8,128)S(1)}) fusion(f32[6,512,512]{1,2,0:T(8,128)} %get-tuple-element.13, f32[6,512]{1,0:T(8,128)S(1)} %get-tuple-element.12, bf16[512,6,128]{0,2,1:T(8,128)(2,1)} %bitcast.115, bf16[512,1152]{1,0:T(8,128)(2,1)} %bitcast.104), kind=kOutput, calls=%fused_computation.3 | convolution fusion | flops 407368704 | bytes 13524992 | tf_op jit(solution)/shard_map/qrd,kd->rqk/dot_general | solution.py:58
  166.6 0.6 slice-done.1
  167.2 1.8 fusion.3
  169.0 1.6 copy-done.1
  170.6 1.6 fusion.15
  172.2 0.2 concatenate.14
  172.5 2.9 %fusion.23 = bf16[512,128]{1,0:T(8,128)(2,1)S(1)} fusion(bf16[6,512,512]{1,2,0:T(8,128)(2,1)} %copy-done.1, bf16[512,6,128]{0,2,1:T(8,128)(2,1)S(1)} %bitcast.112), kind=kOutput, calls=%fused_computation.28 | convolution fusion | flops 402784256 | bytes 4063232 | tf_op jit(solution)/shard_map/rqk,qrd->kd/dot_general | solution.py:62
  175.5 1.0 pad_maximum_fusion
  176.6 3.5 %all-to-all-start.1 = ((bf16[4,128,1024]{1,2,0:T(8,128)(2,1)}), bf16[4,128,1024]{1,2,0:T(8,128)(2,1)S(1)}, u32[]{:S(2)}, u32[]{:S(2)}) async-start(bf16[4,128,1024]{1,2,0:T(8,128)(2,1)} %pad_maximum_fusion), calls=%async_computation.2 | async-start | bytes 2097152 | tf_op jit(solution)/shard_map/all_to_all | solution.py:65
  180.1 6.9 %convolution_convert_fusion.2 = bf16[512,768]{1,0:T(8,128)(2,1)} fusion(bf16[512,3072]{0,1:T(8,128)(2,1)} %all-gather.3.cloned.1.call-done, bf16[3072,768]{1,0:T(8,128)(2,1)} %all-gather.5.cloned.1.call-done), kind=kOutput, calls=%fused_computation.21 | convolution fusion | flops 2416312320 | bytes 8650752 | tf_op jit(solution)/shard_map/dot_general | solution.py:69
  187.0 26.4 %reduce-scatter.5.cloned.1.call-done = bf16[384,768]{1,0:T(8,128)(2,1)} async-done(((bf16[3072,768]{1,0:T(8,128)(2,1)}), bf16[384,768]{1,0:T(8,128)(2,1)}) %reduce-scatter.5.cloned.1.call-update) | async-done | bytes 589840 | tf_op jit(solution)/shard_map/reduce_scatter | solution.py:52
  213.4 2.2 convert_element_type.62
  215.7 1.2 copy.59
  216.8 0.8 copy.61
  217.6 0.8 copy.60
  (31 shorter events, 1.0 us)
Async XLA Ops:
  7.2 56.9 %copy-start = (bf16[512,768]{1,0:T(8,128)(2,1)S(1)}, bf16[512,768]{1,0:T(8,128)(2,1)}, u32[]{:S(2)}) copy-start(bf16[512,768]{1,0:T(8,128)(2,1)} %param.11) | copy-start | bytes 2359300
  7.2 56.9 %all-gather.5.cloned.1.call-start = ((), (), s32[]{:S(2)}) async-start(), calls=%async_computation.5 | async-start | bytes 5308416 | tf_op jit(solution)/shard_map/all_gather | solution.py:23
  7.9 101.4 %all-gather.3.cloned.1.call-start = ((), (), s32[]{:S(2)}) async-start(), calls=%async_computation.4 | async-start | bytes 3932160 | tf_op jit(solution)/shard_map/all_gather | solution.py:48
  31.6 6.1 %copy-start.2 = (bf16[4,128,1152]{2,1,0:T(8,128)(2,1)}, bf16[4,128,1152]{2,1,0:T(8,128)(2,1)S(1)}, u32[]{:S(2)}) copy-start(bf16[4,128,1152]{2,1,0:T(8,128)(2,1)S(1)} %all_to_all.10) | copy-start | bytes 3538948
  31.9 5.8 %copy-start.3 = (bf16[512,768]{0,1:T(8,128)(2,1)}, bf16[512,768]{0,1:T(8,128)(2,1)S(1)}, u32[]{:S(2)}) copy-start(bf16[512,768]{0,1:T(8,128)(2,1)S(1)} %copy.46) | copy-start | bytes 2359300
  42.1 114.2 %reduce-scatter.3.cloned.1.call-start = ((), (), s32[]{:S(2)}) async-start(), calls=%async_computation.6 | async-start | bytes 3932160 | tf_op jit(solution)/shard_map/reduce_scatter | solution.py:56
  70.4 143.0 %reduce-scatter.5.cloned.1.call-start = ((), (), s32[]{:S(2)}) async-start(), calls=%async_computation.7 | async-start | bytes 5308416 | tf_op jit(solution)/shard_map/reduce_scatter | solution.py:52
  157.7 4.1 %copy-start.5 = (bf16[512,768]{0,1:T(8,128)(2,1)}, bf16[512,768]{0,1:T(8,128)(2,1)S(1)}, u32[]{:S(2)}) copy-start(bf16[512,768]{0,1:T(8,128)(2,1)S(1)} %copy.50) | copy-start | bytes 2359300
  161.8 4.8 %slice-start = ((s8[6291456]{0:T(1024)(128)(4,1)}), s8[2097152]{0:T(1024)(128)(4,1)S(1)}, s32[]{:S(2)}) async-start(s8[6291456]{0:T(1024)(128)(4,1)} %bitcast.98), calls=%async_computation.8 | async-start | bytes 4194304
  162.0 5.2 %slice-start.1 = ((s8[6291456]{0:T(1024)(128)(4,1)}), s8[4194304]{0:T(1024)(128)(4,1)S(1)}, s32[]{:S(2)}) async-start(s8[6291456]{0:T(1024)(128)(4,1)} %bitcast.98), calls=%async_computation.9 | async-start | bytes 8388608
  169.0 1.6 copy-start.1
  170.6 1.9 copy-start.4
  176.6 39.0 %all-to-all-start.1 = ((bf16[4,128,1024]{1,2,0:T(8,128)(2,1)}), bf16[4,128,1024]{1,2,0:T(8,128)(2,1)S(1)}, u32[]{:S(2)}, u32[]{:S(2)}) async-start(bf16[4,128,1024]{1,2,0:T(8,128)(2,1)} %pad_maximum_fusion), calls=%async_computation.2 | async-start | bytes 2097152 | tf_op jit(solution)/shard_map/all_to_all | solution.py:65
Sparse Core Ops, SparseCore 0:
  9.7 54.3 all-gather.4
  66.5 42.7 all-gather.2
  112.3 43.9 reduce-scatter.2
  158.5 54.9 reduce-scatter.4

commit v2 on v1

v2 whole, which is shorter than its diff:
```python
import functools
import math

import jax
import jax.numpy as jnp
from jax import lax
from jax.experimental import pallas as pl
from jax.experimental.pallas import tpu as pltpu
from jax.sharding import PartitionSpec as P

HQ = 24
HK = 4
HD = 128
SCALE = 1.0 / math.sqrt(HD)
MESH = pl.DeviceIdType.MESH
F32 = jnp.float32
BF16 = jnp.bfloat16


def dot_nt(a, b):
    return lax.dot_general(a, b, (((1,), (1,)), ((), ())), preferred_element_type=F32)


def dot_tn(a, b):
    return lax.dot_general(a, b, (((0,), (0,)), ((), ())), preferred_element_type=F32)


def dot_nn(a, b):
    return jnp.dot(a, b, preferred_element_type=F32)


def kernel(
    n_dp, n_cp,
    q_ref, k_ref, v_ref, seg_ref, w_ref, go_ref,
    out_ref, dq_ref, dk_ref, dv_ref, dw_ref,
    qh, kh, vh, sg, bias, w_all, att, wp, sib, fr, fl, gas, gar, gsum, dqs, dqr, dka, dva, kvs, kvr,
    in_s, in_r, wr_s, wr_r, wl_s, wl_r, ws_s, ws_r, att_s, att_r, ga_s, ga_r,
    sb_s, sb_r, fr_s, fr_r, fl_s, fl_r, dq_s, dq_r, kv_s, kv_r,
):
    d = lax.axis_index("dp")
    c = lax.axis_index("cp")
    nz = n_dp // 2
    z = d // 2
    core = lax.rem(d, 2)
    sibling = d + 1 - 2 * core
    rows = q_ref.shape[0]
    group = rows * n_cp
    width = q_ref.shape[1] // n_cp
    share = width // HD
    copies = n_cp // HK
    shard, cols = w_ref.shape
    has_left = z > 0
    has_right = z < nz - 1
    pending = []

    def remote(src, dst, send, recv, dp, cp):
        return pltpu.make_async_remote_copy(
            src_ref=src, dst_ref=dst, send_sem=send, recv_sem=recv,
            device_id=(dp, cp), device_id_type=MESH,
        )

    def start(cond, make):
        pending.append((cond, make))
        if cond is None:
            make().start()
        else:
            pl.when(cond)(lambda: make().start())

    def wait_recv(cond, make):
        if cond is None:
            make().wait_recv()
        else:
            pl.when(cond)(lambda: make().wait_recv())

    barrier = pltpu.get_barrier_semaphore()

    def greet(dp, cp):
        pl.semaphore_signal(barrier, inc=1, device_id=(dp, cp), device_id_type=MESH)

    for j in range(1, n_cp):
        greet(d, lax.rem(c + j, n_cp))
    greet(sibling, c)
    pl.when(has_left)(lambda: greet(d - 2, c))
    pl.when(has_right)(lambda: greet(d + 2, c))
    pl.semaphore_wait(barrier, n_cp + jnp.where(has_left, 1, 0) + jnp.where(has_right, 1, 0))

    def w_right(s):
        slot = jnp.maximum(2 * (z - s) + core, 0)
        return remote(w_all.at[slot], w_all.at[slot], wr_s.at[s], wr_r.at[s], d + 2, c)

    def w_left(s):
        slot = jnp.minimum(2 * (z + s) + core, n_dp - 1)
        return remote(w_all.at[slot], w_all.at[slot], wl_s.at[s], wl_r.at[s], d - 2, c)

    def w_sib(slot, i):
        return remote(w_all.at[slot], w_all.at[slot], ws_s.at[i], ws_r.at[i], sibling, c)

    def row_slice(b):
        return pl.ds(pl.multiple_of(b * rows, rows), rows)

    def in_copies(j):
        peer = lax.rem(c + j, n_cp)
        qc = pl.ds(pl.multiple_of(peer * width, HD), width)
        kc = pl.ds(pl.multiple_of((peer // copies) * HD, HD), HD)
        mine = row_slice(c)
        pairs = (
            (q_ref.at[:, qc], qh.at[mine]),
            (k_ref.at[:, kc], kh.at[mine]),
            (v_ref.at[:, kc], vh.at[mine]),
            (seg_ref, sg.at[c]),
        )
        return [
            functools.partial(remote, a, b, in_s.at[i, j], in_r.at[i, j], d, peer)
            for i, (a, b) in enumerate(pairs)
        ]

    for j in range(1, n_cp):
        for make in in_copies(j):
            start(None, make)
    w_all[d] = w_ref[...]
    start(has_right, functools.partial(w_right, 0))
    start(has_left, functools.partial(w_left, 0))
    start(None, functools.partial(w_sib, d, 0))

    own_q = pl.ds(pl.multiple_of(c * width, HD), width)
    own_k = pl.ds(pl.multiple_of((c // copies) * HD, HD), HD)
    qh[row_slice(c), :] = q_ref[:, own_q]
    kh[row_slice(c), :] = k_ref[:, own_k]
    vh[row_slice(c), :] = v_ref[:, own_k]
    sg[c] = seg_ref[...]

    def ga_copy(t):
        return remote(
            gas.at[t], gar.at[c], ga_s.at[t], ga_r.at[lax.rem(t - c + n_cp, n_cp)], d, t
        )

    def ga_unit(t):
        def body(b, carry):
            unit = w_all[pl.ds(2 * t, 2)].reshape(2 * shard, cols)
            gas[t, row_slice(b), :] = dot_nt(go_ref[row_slice(b), :], unit).astype(BF16)
            return carry

        lax.fori_loop(0, n_cp, body, 0)

        @pl.when(t == c)
        def _():
            gar[c] = gas[t]

        @pl.when(t != c)
        def _():
            ga_copy(t).start()

    def gather_step(s):
        left_on, right_on = z - 1 - s >= 0, z + 1 + s < nz
        wait_recv(left_on, functools.partial(w_right, s))
        wait_recv(right_on, functools.partial(w_left, s))
        if s + 1 < nz - 1:
            start(left_on & has_right, functools.partial(w_right, s + 1))
            start(right_on & has_left, functools.partial(w_left, s + 1))
        lslot = jnp.maximum(2 * (z - 1 - s) + core, 0)
        rslot = jnp.minimum(2 * (z + 1 + s) + core, n_dp - 1)
        start(left_on, functools.partial(w_sib, lslot, 1 + s))
        start(right_on, functools.partial(w_sib, rslot, nz + s))

    def gather_use(s):
        for on, i, t in ((z - 1 - s >= 0, 1 + s, z - 1 - s), (z + 1 + s < nz, nz + s, z + 1 + s)):

            @pl.when(on)
            def _(i=i, t=t):
                w_sib(d, i).wait_recv()
                ga_unit(t)

    for j in range(1, n_cp):
        for make in in_copies(j):
            wait_recv(None, make)

    ones = jnp.ones((8, HD), BF16)
    for b in range(n_cp):
        at = slice(b * rows, (b + 1) * rows)
        seg_col = dot_tn(sg[b].astype(F32).astype(BF16), ones)[:, :1] * 0.125
        seg_row = jnp.concatenate([sg[e][:1, :] for e in range(n_cp)], axis=1).astype(F32)
        i = lax.broadcasted_iota(jnp.int32, (rows, group), 0) + b * rows
        jj = lax.broadcasted_iota(jnp.int32, (rows, group), 1)
        bias[at, :] = jnp.where((jj <= i) & (seg_col == seg_row), 0.0, -1e30)

    def probability(b, col):
        last = (b + 1) * rows
        q = qh[b * rows : last, col]
        s = dot_nt(q, kh[:last, :]) * SCALE + bias[b * rows : last, :last]
        e = jnp.exp(s - jnp.max(s, axis=1, keepdims=True))
        return q, e / jnp.sum(e, axis=1, keepdims=True)

    def head_col(r):
        return pl.ds(pl.multiple_of(r * HD, HD), HD)

    def forward(b):
        def body(r, carry):
            col = head_col(r)
            _, p = probability(b, col)
            a = dot_nn(p.astype(BF16), vh[: (b + 1) * rows, :]).astype(BF16)
            att[c, b * rows : (b + 1) * rows, col] = a
            return carry

        lax.fori_loop(0, share, body, 0)

    half = group // 2

    def att_copy(j, h):
        part = att.at[c, pl.ds(h * half, half)]
        return remote(part, part, att_s.at[h, j], att_r.at[h, j], d, lax.rem(c + j, n_cp))

    for h in range(2):
        for b in range(h * n_cp // 2, (h + 1) * n_cp // 2):
            forward(b)
        for j in range(1, n_cp):
            start(None, functools.partial(att_copy, j, h))
        if h == 0:
            gather_step(0)
    w_sib(d, 0).wait_recv()
    ga_unit(z)
    gather_use(0)
    if nz > 2:
        gather_step(1)

    def sib_copy(t):
        return remote(
            wp.at[2 * t + 1 - core], sib.at[t], sb_s.at[t], sb_r.at[t], sibling, c
        )

    def weight_unit(j, carry):
        t = lax.rem(c - j + n_cp, n_cp)

        @pl.when(j > 0)
        def _():
            att_copy(j, 0).wait_recv()
            att_copy(j, 1).wait_recv()

        part = dot_tn(att[t], go_ref[...]).astype(BF16)
        wp[pl.ds(2 * t, 2)] = part.reshape(2, shard, cols)
        sib_copy(t).start()
        return carry

    lax.fori_loop(0, n_cp, weight_unit, 0)

    def right_copy(s):
        t = nz - 1 - s
        return remote(wp.at[2 * t + core], fr.at[s], fr_s.at[s], fr_r.at[s], d + 2, c)

    def left_copy(s):
        return remote(wp.at[2 * s + core], fl.at[s], fl_s.at[s], fl_r.at[s], d - 2, c)

    def reduce_step(s):
        for t, on, has, make, arrived in (
            (nz - 1 - s, z < nz - 1 - s, has_left, right_copy, fr),
            (s, z > s, has_right, left_copy, fl),
        ):

            @pl.when(on)
            def _(t=t, has=has, make=make, arrived=arrived):
                sib_copy(t).wait_recv()
                mine = 2 * t + core

                @pl.when(has)
                def _():
                    make(s).wait_recv()
                    total = wp[mine].astype(F32) + sib[t].astype(F32) + arrived[s].astype(F32)
                    wp[mine] = total.astype(BF16)

                @pl.when(jnp.logical_not(has))
                def _():
                    wp[mine] = (wp[mine].astype(F32) + sib[t].astype(F32)).astype(BF16)

                make(s).start()

            pending.append((on, functools.partial(make, s)))

    for s in range(nz - 1):
        reduce_step(s)
        if s == 0:
            if nz > 2:
                gather_use(1)
            for e in range(2, nz - 1):
                gather_step(e)
                gather_use(e)
        if s == 1:
            output(n_cp, att, w_all, out_ref, row_slice, shard, cols)

    for j in range(1, n_cp):
        peer = lax.rem(c + j, n_cp)
        remote(gas.at[peer], gar.at[c], ga_s.at[peer], ga_r.at[j], d, peer).wait_recv()

    def sum_ga(b, carry):
        at = row_slice(b)
        total = gar[0, at, :].astype(F32)
        for e in range(1, n_cp):
            total = total + gar[e, at, :].astype(F32)
        gsum[at, :] = total.astype(BF16)
        return carry

    lax.fori_loop(0, n_cp, sum_ga, 0)
    dka[...] = jnp.zeros_like(dka)
    dva[...] = jnp.zeros_like(dva)

    def dq_copy(b):
        return remote(
            dqs.at[b], dqr.at[c], dq_s.at[b], dq_r.at[lax.rem(b - c + n_cp, n_cp)], d, b
        )

    def kv_copy(b):
        return remote(
            kvs.at[b], kvr.at[c], kv_s.at[b], kv_r.at[lax.rem(b - c + n_cp, n_cp)], d, b
        )

    def send_back(b, source, target, make):
        @pl.when(c == b)
        def _():
            target[c] = source[b]

        start(c != b, functools.partial(make, b))

    for b in reversed(range(n_cp)):
        last = (b + 1) * rows

        def body(r, carry, b=b, last=last):
            col = head_col(r)
            q, p = probability(b, col)
            g = gsum[b * rows : last, col]
            gp = dot_nt(g, vh[:last, :])
            delta = jnp.sum(p * gp, axis=1, keepdims=True)
            ds = (p * (gp - delta)).astype(BF16)
            dqs[b, :, col] = (dot_nn(ds, kh[:last, :]) * SCALE).astype(BF16)
            dka[:last, :] += dot_tn(ds, q)
            dva[:last, :] += dot_tn(p.astype(BF16), g)
            return carry

        lax.fori_loop(0, share, body, 0)
        send_back(b, dqs, dqr, dq_copy)
    for b in range(n_cp):
        at = slice(b * rows, (b + 1) * rows)
        kvs[b, :, :HD] = (dka[at, :] * SCALE).astype(BF16)
        kvs[b, :, HD:] = dva[at, :].astype(BF16)
        send_back(b, kvs, kvr, kv_copy)

    sib_copy(z).wait_recv()
    dw_ref[...] = wp[2 * z + core].astype(F32) + sib[z].astype(F32)

    @pl.when(has_left)
    def _():
        s = jnp.minimum(nz - 1 - z, nz - 2)
        remote(wp.at[d], fr.at[s], fr_s.at[s], fr_r.at[s], d + 2, c).wait_recv()
        dw_ref[...] += fr[s].astype(F32)

    @pl.when(has_right)
    def _():
        s = jnp.minimum(z, nz - 2)
        remote(wp.at[d], fl.at[s], fl_s.at[s], fl_r.at[s], d - 2, c).wait_recv()
        dw_ref[...] += fl[s].astype(F32)

    for j in range(1, n_cp):
        peer = lax.rem(c + j, n_cp)
        remote(dqs.at[peer], dqr.at[c], dq_s.at[peer], dq_r.at[j], d, peer).wait_recv()
        remote(kvs.at[peer], kvr.at[c], kv_s.at[peer], kv_r.at[j], d, peer).wait_recv()
    for e in range(n_cp):
        dq_ref[:, e * width : (e + 1) * width] = dqr[e]
    for h in range(HK):
        total = kvr[h * copies].astype(F32)
        for e in range(1, copies):
            total = total + kvr[h * copies + e].astype(F32)
        dk_ref[:, h * HD : (h + 1) * HD] = total[:, :HD].astype(BF16)
        dv_ref[:, h * HD : (h + 1) * HD] = total[:, HD:].astype(BF16)

    for cond, make in pending:
        if cond is None:
            make().wait_send()
        else:
            pl.when(cond)(functools.partial(lambda m: m().wait_send(), make))
    for t in range(n_cp):
        pl.when(c != t)(functools.partial(lambda t: ga_copy(t).wait_send(), t))
        sib_copy(t).wait_send()


def output(n_cp, att, w_all, out_ref, row_slice, shard, cols):
    def body(b, carry):
        at = row_slice(b)
        total = jnp.zeros((out_ref.shape[0] // n_cp, cols), F32)
        for t in range(n_cp):
            unit = w_all[2 * t : 2 * t + 2].reshape(2 * shard, cols)
            total = total + dot_nn(att[t, at, :], unit)
        out_ref[at, :] = total.astype(BF16)
        return carry

    lax.fori_loop(0, n_cp, body, 0)


def per_device(n_dp, n_cp, queries, key_heads, value_heads, segment_ids, out_weight, grad_out):
    rows = queries.shape[0]
    group = rows * n_cp
    width = queries.shape[1] // n_cp
    shard, cols = out_weight.shape
    nz = n_dp // 2
    segments = jnp.broadcast_to(segment_ids, (8, rows))
    vmem = pl.BlockSpec(memory_space=pltpu.VMEM)
    dma = pltpu.SemaphoreType.DMA
    block = jax.ShapeDtypeStruct
    return pl.pallas_call(
        functools.partial(kernel, n_dp, n_cp),
        out_shape=(
            block((group, cols), BF16),
            block(queries.shape, BF16),
            block(key_heads.shape, BF16),
            block(value_heads.shape, BF16),
            block((shard, cols), F32),
        ),
        in_specs=[vmem] * 6,
        out_specs=[vmem] * 5,
        scratch_shapes=[
            pltpu.VMEM((group, width), BF16),
            pltpu.VMEM((group, HD), BF16),
            pltpu.VMEM((group, HD), BF16),
            pltpu.VMEM((n_cp, 8, rows), jnp.int32),
            pltpu.VMEM((group, group), F32),
            pltpu.VMEM((n_dp, shard, cols), BF16),
            pltpu.VMEM((n_cp, group, width), BF16),
            pltpu.VMEM((n_dp, shard, cols), BF16),
            pltpu.VMEM((nz, shard, cols), BF16),
            pltpu.VMEM((nz - 1, shard, cols), BF16),
            pltpu.VMEM((nz - 1, shard, cols), BF16),
            pltpu.VMEM((n_cp, group, width), BF16),
            pltpu.VMEM((n_cp, group, width), BF16),
            pltpu.VMEM((group, width), BF16),
            pltpu.VMEM((n_cp, rows, width), BF16),
            pltpu.VMEM((n_cp, rows, width), BF16),
            pltpu.VMEM((group, HD), F32),
            pltpu.VMEM((group, HD), F32),
            pltpu.VMEM((n_cp, rows, 2 * HD), BF16),
            pltpu.VMEM((n_cp, rows, 2 * HD), BF16),
            dma((4, n_cp)), dma((4, n_cp)),
            dma((nz - 1,)), dma((nz - 1,)), dma((nz - 1,)), dma((nz - 1,)),
            dma((2 * nz - 1,)), dma((2 * nz - 1,)),
            dma((2, n_cp)), dma((2, n_cp)),
            dma((n_cp,)), dma((n_cp,)),
            dma((nz,)), dma((nz,)),
            dma((nz - 1,)), dma((nz - 1,)), dma((nz - 1,)), dma((nz - 1,)),
            dma((n_cp,)), dma((n_cp,)), dma((n_cp,)), dma((n_cp,)),
        ],
        compiler_params=pltpu.CompilerParams(
            collective_id=0, has_side_effects=True, vmem_limit_bytes=60 * 1024 * 1024
        ),
    )(queries, key_heads, value_heads, segments, out_weight, grad_out)


def solution(mesh):
    rows = P(("dp", "cp"), None)
    grid = P("dp", "cp")
    return jax.shard_map(
        functools.partial(per_device, mesh.shape["dp"], mesh.shape["cp"]),
        mesh=mesh,
        in_specs=(rows, rows, rows, grid, grid, grid),
        out_specs=(grid, rows, rows, rows, grid),
        check_vma=False,
    )
```

time: 225 us -> 181 us (0.80)
  the two profiles are of different devices: /device:TPU:0 before, /device:TPU:8 now
where the time goes in v2:
time: 181 us
  Pallas kernels  174 us (96%)
  local copies, waits for them, and re-layouts  6.71 us (4%)
    pallas_call x1, Pallas kernels, per_device(): pl.pallas_call(functools.partial(kernel, n_dp, n_cp), out_shape=(block((g...  174 us
    unnamed x13, local copies, waits for them, and re-layouts  5.46 us

profile of v2, /device:TPU:8, one launch (start us, length us, event | category | flops | bytes accessed | tf_op | source)
XLA Modules:
  0.0 181.0 jit_solution(4657868364904945136)
XLA Ops:
  0.6 1.2 broadcast_in_dim.8.seg_ref
  1.9 173.6 %shard_map.101 = (bf16[512,768]{1,0:T(8,128)(2,1)}, bf16[128,3072]{1,0:T(8,128)(2,1)}, bf16[128,512]{1,0:T(8,128)(2,1)}, bf16[128,512]{1,0:T(8,128)(2,1)}, f32[384,768]{1,0:T(8,128)}) custom-call(bf16[128,3072]{1,0:T(8,128)(2,1)} %q_ref.1, bf16[128,512]{1,0:T(8,128)(2,1)} %k_ref.1, bf16[128,512]{1,0:T(8,128)(2,1)} %v_ref.1, ...), custom_call_target="tpu_custom_call" | custom-call | tf_op jit(solution)/shard_map/pallas_call | solution.py:405
  175.5 0.0 copy-start.1
  175.5 2.1 %copy.16 = bf16[512,768]{1,0:T(8,128)(2,1)} copy(bf16[512,768]{1,0:T(8,128)(2,1)} %get-tuple-element.10) | data formatting | bytes 1572864
  177.7 0.0 copy-done.1
  177.7 0.0 copy-start.3
  177.7 0.0 copy-start.2
  177.7 0.0 copy-start
  177.7 0.9 copy.17
  178.6 0.1 copy-done.3
  178.7 0.7 copy.18
  179.3 0.0 copy-done.2
  179.3 0.7 copy.19
  180.0 0.0 copy-done
  180.0 1.0 copy.20
Async XLA Ops:
  175.5 2.1 %copy-start.1 = (bf16[128,3072]{1,0:T(8,128)(2,1)S(1)}, bf16[128,3072]{1,0:T(8,128)(2,1)}, u32[]{:S(2)}) copy-start(bf16[128,3072]{1,0:T(8,128)(2,1)} %get-tuple-element.11) | copy-start | bytes 2359300
  177.7 1.0 copy-start.3
  177.7 1.7 copy-start.2
  177.7 2.3 %copy-start = (f32[384,768]{1,0:T(8,128)S(1)}, f32[384,768]{1,0:T(8,128)}, u32[]{:S(2)}) copy-start(f32[384,768]{1,0:T(8,128)} %get-tuple-element.14) | copy-start | bytes 3538948

commit v3 on v2

--- a/solution.py
+++ b/solution.py
@@ -221,6 +221,7 @@
     gather_use(0)
     if nz > 2:
         gather_step(1)
+        gather_use(1)
 
     def sib_copy(t):
         return remote(
@@ -249,14 +250,15 @@
     def left_copy(s):
         return remote(wp.at[2 * s + core], fl.at[s], fl_s.at[s], fl_r.at[s], d - 2, c)
 
-    def reduce_step(s):
-        for t, on, has, make, arrived in (
-            (nz - 1 - s, z < nz - 1 - s, has_left, right_copy, fr),
-            (s, z > s, has_right, left_copy, fl),
+    def reduce_step(time):
+        right, left = time - z, time - (nz - 1 - z)
+        for s, t, has, make, arrived in (
+            (right, nz - 1 - right, has_left, right_copy, fr),
+            (left, left, has_right, left_copy, fl),
         ):
 
-            @pl.when(on)
-            def _(t=t, has=has, make=make, arrived=arrived):
+            @pl.when(s >= 0)
+            def _(s=s, t=t, has=has, make=make, arrived=arrived):
                 sib_copy(t).wait_recv()
                 mine = 2 * t + core
 
@@ -272,17 +274,15 @@
 
                 make(s).start()
 
-            pending.append((on, functools.partial(make, s)))
-
-    for s in range(nz - 1):
-        reduce_step(s)
-        if s == 0:
-            if nz > 2:
-                gather_use(1)
-            for e in range(2, nz - 1):
-                gather_step(e)
-                gather_use(e)
-        if s == 1:
+            pending.append((s >= 0, functools.partial(make, s)))
+
+    reduce_step(0)
+    for e in range(2, nz - 1):
+        gather_step(e)
+        gather_use(e)
+    for time in range(1, nz - 1):
+        reduce_step(time)
+        if time == 1:
             output(n_cp, att, w_all, out_ref, row_slice, shard, cols)
 
     for j in range(1, n_cp):

time: 181 us -> 149 us (0.82)
  the two profiles are of different devices: /device:TPU:8 before, /device:TPU:0 now
where the time goes in v3:
time: 149 us
  Pallas kernels  142 us (95%)
  local copies, waits for them, and re-layouts  6.71 us (5%)
    pallas_call x1, Pallas kernels, per_device(): pl.pallas_call(functools.partial(kernel, n_dp, n_cp), out_shape=(block((g...  142 us
    unnamed x13, local copies, waits for them, and re-layouts  5.46 us

profile of v3, /device:TPU:0, one launch (start us, length us, event | category | flops | bytes accessed | tf_op | source)
XLA Modules:
  0.0 149.2 jit_solution(14004847128051577247)
XLA Ops:
  0.6 1.2 broadcast_in_dim.8.seg_ref
  1.9 141.9 %shard_map.101 = (bf16[512,768]{1,0:T(8,128)(2,1)}, bf16[128,3072]{1,0:T(8,128)(2,1)}, bf16[128,512]{1,0:T(8,128)(2,1)}, bf16[128,512]{1,0:T(8,128)(2,1)}, f32[384,768]{1,0:T(8,128)}) custom-call(bf16[128,3072]{1,0:T(8,128)(2,1)} %q_ref.1, bf16[128,512]{1,0:T(8,128)(2,1)} %k_ref.1, bf16[128,512]{1,0:T(8,128)(2,1)} %v_ref.1, ...), custom_call_target="tpu_custom_call" | custom-call | tf_op jit(solution)/shard_map/pallas_call | solution.py:405
  143.7 0.0 copy-start.1
  143.8 2.1 %copy.16 = bf16[512,768]{1,0:T(8,128)(2,1)} copy(bf16[512,768]{1,0:T(8,128)(2,1)} %get-tuple-element.10) | data formatting | bytes 1572864
  145.9 0.0 copy-done.1
  145.9 0.0 copy-start.3
  145.9 0.0 copy-start.2
  145.9 0.0 copy-start
  145.9 0.9 copy.17
  146.8 0.1 copy-done.3
  146.9 0.7 copy.18
  147.5 0.0 copy-done.2
  147.6 0.7 copy.19
  148.2 0.0 copy-done
  148.2 1.0 copy.20
Async XLA Ops:
  143.7 2.1 %copy-start.1 = (bf16[128,3072]{1,0:T(8,128)(2,1)S(1)}, bf16[128,3072]{1,0:T(8,128)(2,1)}, u32[]{:S(2)}) copy-start(bf16[128,3072]{1,0:T(8,128)(2,1)} %get-tuple-element.11) | copy-start | bytes 2359300
  145.9 1.0 copy-start.3
  145.9 1.7 %copy-start.2 = (bf16[128,512]{1,0:T(8,128)(2,1)S(1)}, bf16[128,512]{1,0:T(8,128)(2,1)}, u32[]{:S(2)}) copy-start(bf16[128,512]{1,0:T(8,128)(2,1)} %get-tuple-element.13) | copy-start | bytes 393220
  145.9 2.3 %copy-start = (f32[384,768]{1,0:T(8,128)S(1)}, f32[384,768]{1,0:T(8,128)}, u32[]{:S(2)}) copy-start(f32[384,768]{1,0:T(8,128)} %get-tuple-element.14) | copy-start | bytes 3538948

commit v4 on v3

--- a/solution.py
+++ b/solution.py
@@ -33,7 +33,7 @@
     n_dp, n_cp,
     q_ref, k_ref, v_ref, seg_ref, w_ref, go_ref,
     out_ref, dq_ref, dk_ref, dv_ref, dw_ref,
-    qh, kh, vh, sg, bias, w_all, att, wp, sib, fr, fl, gas, gar, gsum, dqs, dqr, dka, dva, kvs, kvr,
+    qh, kh, vh, sg, bias, w_all, att, wp, sib, fr, fl, gas, gar, gsum, dqs, dqr, dka, dva, kvs, kvr, prob,
     in_s, in_r, wr_s, wr_r, wl_s, wl_r, ws_s, ws_r, att_s, att_r, ga_s, ga_r,
     sb_s, sb_r, fr_s, fr_r, fl_s, fl_r, dq_s, dq_r, kv_s, kv_r,
 ):
@@ -129,10 +129,13 @@
     vh[row_slice(c), :] = v_ref[:, own_k]
     sg[c] = seg_ref[...]
 
-    def ga_copy(t):
-        return remote(
-            gas.at[t], gar.at[c], ga_s.at[t], ga_r.at[lax.rem(t - c + n_cp, n_cp)], d, t
-        )
+    half = group // 2
+    half_blocks = n_cp // 2
+
+    def ga_copy(t, h):
+        part = pl.ds(h * half, half)
+        j = lax.rem(t - c + n_cp, n_cp)
+        return remote(gas.at[t, part], gar.at[c, part], ga_s.at[h, t], ga_r.at[h, j], d, t)
 
     def ga_unit(t):
         def body(b, carry):
@@ -140,15 +143,16 @@
             gas[t, row_slice(b), :] = dot_nt(go_ref[row_slice(b), :], unit).astype(BF16)
             return carry
 
-        lax.fori_loop(0, n_cp, body, 0)
+        for h in (1, 0):
+            lax.fori_loop(h * half_blocks, (h + 1) * half_blocks, body, 0)
+
+            @pl.when(t != c)
+            def _(h=h):
+                ga_copy(t, h).start()
 
         @pl.when(t == c)
         def _():
             gar[c] = gas[t]
-
-        @pl.when(t != c)
-        def _():
-            ga_copy(t).start()
 
     def gather_step(s):
         left_on, right_on = z - 1 - s >= 0, z + 1 + s < nz
@@ -170,6 +174,8 @@
                 w_sib(d, i).wait_recv()
                 ga_unit(t)
 
+    w_sib(d, 0).wait_recv()
+    ga_unit(z)
     for j in range(1, n_cp):
         for make in in_copies(j):
             wait_recv(None, make)
@@ -188,7 +194,7 @@
         q = qh[b * rows : last, col]
         s = dot_nt(q, kh[:last, :]) * SCALE + bias[b * rows : last, :last]
         e = jnp.exp(s - jnp.max(s, axis=1, keepdims=True))
-        return q, e / jnp.sum(e, axis=1, keepdims=True)
+        return e / jnp.sum(e, axis=1, keepdims=True)
 
     def head_col(r):
         return pl.ds(pl.multiple_of(r * HD, HD), HD)
@@ -196,14 +202,13 @@
     def forward(b):
         def body(r, carry):
             col = head_col(r)
-            _, p = probability(b, col)
+            p = probability(b, col)
+            prob[r, b * rows : (b + 1) * rows, : (b + 1) * rows] = p
             a = dot_nn(p.astype(BF16), vh[: (b + 1) * rows, :]).astype(BF16)
             att[c, b * rows : (b + 1) * rows, col] = a
             return carry
 
         lax.fori_loop(0, share, body, 0)
-
-    half = group // 2
 
     def att_copy(j, h):
         part = att.at[c, pl.ds(h * half, half)]
@@ -216,8 +221,6 @@
             start(None, functools.partial(att_copy, j, h))
         if h == 0:
             gather_step(0)
-    w_sib(d, 0).wait_recv()
-    ga_unit(z)
     gather_use(0)
     if nz > 2:
         gather_step(1)
@@ -285,10 +288,6 @@
         if time == 1:
             output(n_cp, att, w_all, out_ref, row_slice, shard, cols)
 
-    for j in range(1, n_cp):
-        peer = lax.rem(c + j, n_cp)
-        remote(gas.at[peer], gar.at[c], ga_s.at[peer], ga_r.at[j], d, peer).wait_recv()
-
     def sum_ga(b, carry):
         at = row_slice(b)
         total = gar[0, at, :].astype(F32)
@@ -297,7 +296,6 @@
         gsum[at, :] = total.astype(BF16)
         return carry
 
-    lax.fori_loop(0, n_cp, sum_ga, 0)
     dka[...] = jnp.zeros_like(dka)
     dva[...] = jnp.zeros_like(dva)
 
@@ -320,10 +318,16 @@
 
     for b in reversed(range(n_cp)):
         last = (b + 1) * rows
+        if b in (n_cp - 1, half_blocks - 1):
+            h = b // half_blocks
+            for j in range(1, n_cp):
+                ga_copy(lax.rem(c + j, n_cp), h).wait_recv()
+            lax.fori_loop(h * half_blocks, (h + 1) * half_blocks, sum_ga, 0)
 
         def body(r, carry, b=b, last=last):
             col = head_col(r)
-            q, p = probability(b, col)
+            q = qh[b * rows : last, col]
+            p = prob[r, b * rows : last, :last]
             g = gsum[b * rows : last, col]
             gp = dot_nt(g, vh[:last, :])
             delta = jnp.sum(p * gp, axis=1, keepdims=True)
@@ -375,7 +379,8 @@
         else:
             pl.when(cond)(functools.partial(lambda m: m().wait_send(), make))
     for t in range(n_cp):
-        pl.when(c != t)(functools.partial(lambda t: ga_copy(t).wait_send(), t))
+        for h in range(2):
+            pl.when(c != t)(functools.partial(lambda t, h: ga_copy(t, h).wait_send(), t, h))
         sib_copy(t).wait_send()
 
 
@@ -434,11 +439,12 @@
             pltpu.VMEM((group, HD), F32),
             pltpu.VMEM((n_cp, rows, 2 * HD), BF16),
             pltpu.VMEM((n_cp, rows, 2 * HD), BF16),
+            pltpu.VMEM((width // HD, group, group), F32),
             dma((4, n_cp)), dma((4, n_cp)),
             dma((nz - 1,)), dma((nz - 1,)), dma((nz - 1,)), dma((nz - 1,)),
             dma((2 * nz - 1,)), dma((2 * nz - 1,)),
             dma((2, n_cp)), dma((2, n_cp)),
-            dma((n_cp,)), dma((n_cp,)),
+            dma((2, n_cp)), dma((2, n_cp)),
             dma((nz,)), dma((nz,)),
             dma((nz - 1,)), dma((nz - 1,)), dma((nz - 1,)), dma((nz - 1,)),
             dma((n_cp,)), dma((n_cp,)), dma((n_cp,)), dma((n_cp,)),

time: 149 us -> 149 us (level)
  no operation moved by 1% of the time
where the time goes in v4:
time: 149 us
  Pallas kernels  141 us (95%)
  local copies, waits for them, and re-layouts  6.71 us (5%)
    pallas_call x1, Pallas kernels, per_device(): pl.pallas_call(functools.partial(kernel, n_dp, n_cp), out_shape=(block((g...  141 us
    unnamed x13, local copies, waits for them, and re-layouts  5.46 us

profile of v4, /device:TPU:0, one launch (start us, length us, event | category | flops | bytes accessed | tf_op | source)
XLA Modules:
  0.0 148.7 jit_solution(14574529593405414794)
XLA Ops:
  0.6 1.2 broadcast_in_dim.8.seg_ref
  1.9 141.3 %shard_map.101 = (bf16[512,768]{1,0:T(8,128)(2,1)}, bf16[128,3072]{1,0:T(8,128)(2,1)}, bf16[128,512]{1,0:T(8,128)(2,1)}, bf16[128,512]{1,0:T(8,128)(2,1)}, f32[384,768]{1,0:T(8,128)}) custom-call(bf16[128,3072]{1,0:T(8,128)(2,1)} %q_ref.1, bf16[128,512]{1,0:T(8,128)(2,1)} %k_ref.1, bf16[128,512]{1,0:T(8,128)(2,1)} %v_ref.1, ...), custom_call_target="tpu_custom_call" | custom-call | tf_op jit(solution)/shard_map/pallas_call | solution.py:410
  143.2 0.0 copy-start.1
  143.2 2.1 %copy.16 = bf16[512,768]{1,0:T(8,128)(2,1)} copy(bf16[512,768]{1,0:T(8,128)(2,1)} %get-tuple-element.10) | data formatting | bytes 1572864
  145.4 0.0 copy-done.1
  145.4 0.0 copy-start.3
  145.4 0.0 copy-start.2
  145.4 0.0 copy-start
  145.4 0.9 copy.17
  146.3 0.1 copy-done.3
  146.4 0.7 copy.18
  147.0 0.0 copy-done.2
  147.0 0.7 copy.19
  147.7 0.0 copy-done
  147.7 1.0 copy.20
Async XLA Ops:
  143.2 2.1 %copy-start.1 = (bf16[128,3072]{1,0:T(8,128)(2,1)S(1)}, bf16[128,3072]{1,0:T(8,128)(2,1)}, u32[]{:S(2)}) copy-start(bf16[128,3072]{1,0:T(8,128)(2,1)} %get-tuple-element.11) | copy-start | bytes 2359300
  145.4 1.0 copy-start.3
  145.4 1.7 %copy-start.2 = (bf16[128,512]{1,0:T(8,128)(2,1)S(1)}, bf16[128,512]{1,0:T(8,128)(2,1)}, u32[]{:S(2)}) copy-start(bf16[128,512]{1,0:T(8,128)(2,1)} %get-tuple-element.13) | copy-start | bytes 393220
  145.4 2.3 %copy-start = (f32[384,768]{1,0:T(8,128)S(1)}, f32[384,768]{1,0:T(8,128)}, u32[]{:S(2)}) copy-start(f32[384,768]{1,0:T(8,128)} %get-tuple-element.14) | copy-start | bytes 3538948

commit v5 on v4

--- a/solution.py
+++ b/solution.py
@@ -176,6 +176,7 @@
 
     w_sib(d, 0).wait_recv()
     ga_unit(z)
+    gather_step(0)
     for j in range(1, n_cp):
         for make in in_copies(j):
             wait_recv(None, make)
@@ -219,12 +220,10 @@
             forward(b)
         for j in range(1, n_cp):
             start(None, functools.partial(att_copy, j, h))
-        if h == 0:
-            gather_step(0)
-    gather_use(0)
-    if nz > 2:
-        gather_step(1)
-        gather_use(1)
+    for e in range(1, nz - 1):
+        gather_step(e)
+        gather_use(e - 1)
+    gather_use(nz - 2)
 
     def sib_copy(t):
         return remote(
@@ -280,9 +279,6 @@
             pending.append((s >= 0, functools.partial(make, s)))
 
     reduce_step(0)
-    for e in range(2, nz - 1):
-        gather_step(e)
-        gather_use(e)
     for time in range(1, nz - 1):
         reduce_step(time)
         if time == 1:

time: 149 us -> 150 us (level)
  the two profiles are of different devices: /device:TPU:0 before, /device:TPU:12 now
where the time goes in v5:
time: 150 us
  Pallas kernels  143 us (95%)
  local copies, waits for them, and re-layouts  6.71 us (4%)
    pallas_call x1, Pallas kernels, per_device(): pl.pallas_call(functools.partial(kernel, n_dp, n_cp), out_shape=(block((g...  143 us
    unnamed x13, local copies, waits for them, and re-layouts  5.46 us

profile of v5, /device:TPU:12, one launch (start us, length us, event | category | flops | bytes accessed | tf_op | source)
XLA Modules:
  0.0 150.2 jit_solution(1190908230995581097)
XLA Ops:
  0.6 1.2 broadcast_in_dim.8.seg_ref
  1.9 142.8 %shard_map.101 = (bf16[512,768]{1,0:T(8,128)(2,1)}, bf16[128,3072]{1,0:T(8,128)(2,1)}, bf16[128,512]{1,0:T(8,128)(2,1)}, bf16[128,512]{1,0:T(8,128)(2,1)}, f32[384,768]{1,0:T(8,128)}) custom-call(bf16[128,3072]{1,0:T(8,128)(2,1)} %q_ref.1, bf16[128,512]{1,0:T(8,128)(2,1)} %k_ref.1, bf16[128,512]{1,0:T(8,128)(2,1)} %v_ref.1, ...), custom_call_target="tpu_custom_call" | custom-call | tf_op jit(solution)/shard_map/pallas_call | solution.py:406
  144.7 0.0 copy-start.1
  144.7 2.1 %copy.16 = bf16[512,768]{1,0:T(8,128)(2,1)} copy(bf16[512,768]{1,0:T(8,128)(2,1)} %get-tuple-element.10) | data formatting | bytes 1572864
  146.8 0.0 copy-done.1
  146.8 0.0 copy-start.3
  146.8 0.0 copy-start.2
  146.9 0.0 copy-start
  146.9 0.9 copy.17
  147.7 0.1 copy-done.3
  147.8 0.7 copy.18
  148.5 0.0 copy-done.2
  148.5 0.7 copy.19
  149.2 0.0 copy-done
  149.2 1.0 copy.20
Async XLA Ops:
  144.7 2.1 %copy-start.1 = (bf16[128,3072]{1,0:T(8,128)(2,1)S(1)}, bf16[128,3072]{1,0:T(8,128)(2,1)}, u32[]{:S(2)}) copy-start(bf16[128,3072]{1,0:T(8,128)(2,1)} %get-tuple-element.11) | copy-start | bytes 2359300
  146.8 1.0 copy-start.3
  146.8 1.7 %copy-start.2 = (bf16[128,512]{1,0:T(8,128)(2,1)S(1)}, bf16[128,512]{1,0:T(8,128)(2,1)}, u32[]{:S(2)}) copy-start(bf16[128,512]{1,0:T(8,128)(2,1)} %get-tuple-element.13) | copy-start | bytes 393220
  146.9 2.3 %copy-start = (f32[384,768]{1,0:T(8,128)S(1)}, f32[384,768]{1,0:T(8,128)}, u32[]{:S(2)}) copy-start(f32[384,768]{1,0:T(8,128)} %get-tuple-element.14) | copy-start | bytes 3538948
